TPU v7x, 128 devices: a whole 4x4x4 slice. The times are simulated.
128 devices in a mesh: gx: 8 (over x, y_hi), gy: 16 (over z, y_lo, core).
Axes of the slice: x: 4, y: 4 (y_hi: 2, y_lo: 2; y = y_hi * 2 + y_lo), z: 4, core: 2. Of those that a mesh axis runs over, the one named last changes fastest.
Arguments:
- voltages: bfloat16 [2, 2048, 122880], P(None, ('gx', 'gy')), may hold values from -6 to 6
- gains: float32 [2, 2048, 8192], P(None, ('gx', 'gy')), may hold values from -6 to 6
- delays: float32 [64, 2048], replicated, may hold values from -32 to 32
- channel_order: int32 [8, 16], replicated, may hold values from 0 to 15, each once within a row
- beam_table: int32 [64], replicated, may hold values from 0 to 63, each once
Outputs:
- beam_power: float32 [64, 4, 8192], P('gy', None, 'gx')
Inputs may be any that keep to these rules, and one draw needn't show every extreme that they name: Each row names every index of gy once; channel block a * 16 + channel_order[a, b] of 64 channels belongs to the device at gx = a, gy = b. Names every beam once; the beams beam_table[g * 64 / 16] onward, 64 / 16 of them, belong to gy index g.
All inputs are finite; a program needn't handle non-finite values.
Results may differ from a plain program's by a relative error of at most 0.009.
Values may be sent and summed in bfloat16 or wider, within the bound.
A program may use at most 128 MiB of HBM per device.

v0:
```python
import math

import jax
import jax.numpy as jnp
from jax import lax
from jax.sharding import PartitionSpec as P

NIN = 2048
NCH = 8192
NBEAM = 64
TAPS = 8
INTEG = 2
NSPEC = 8
TIMES = 4


def coefficients():
    total = TAPS * NCH
    index = jnp.arange(total, dtype=jnp.float32)
    offset = (index - total / 2) / NCH
    window = 0.5 - 0.5 * jnp.cos(2.0 * math.pi * index / total)
    raw = jnp.sinc(offset) * window
    raw = raw / jnp.sqrt(jnp.sum(raw * raw) / NCH)
    return raw.reshape(TAPS, NCH)


def transform(filtered):
    first_len = 64
    second_len = NCH // first_len
    first_ids = jnp.arange(first_len, dtype=jnp.int32)
    second_ids = jnp.arange(second_len, dtype=jnp.int32)
    small_angle = (
        2.0
        * math.pi
        / first_len
        * (first_ids[:, None] * first_ids[None, :] % first_len).astype(jnp.float32)
    )
    small_cos = jnp.cos(small_angle)
    small_sin = -jnp.sin(small_angle)
    small_stack = jnp.concatenate(
        [
            jnp.concatenate([small_cos, -small_sin], axis=1),
            jnp.concatenate([small_sin, small_cos], axis=1),
        ],
        axis=0,
    ).astype(jnp.bfloat16)
    twist_angle = (
        2.0 * math.pi / NCH * (first_ids[:, None] * second_ids[None, :]).astype(jnp.float32)
    )
    twist_cos = jnp.cos(twist_angle)
    twist_sin = -jnp.sin(twist_angle)
    large_angle = (
        2.0
        * math.pi
        / second_len
        * (second_ids[:, None] * second_ids[None, :] % second_len).astype(jnp.float32)
    )
    large_cos = jnp.cos(large_angle)
    large_sin = -jnp.sin(large_angle)
    large_stack = jnp.concatenate(
        [
            jnp.concatenate([large_cos, large_sin], axis=1),
            jnp.concatenate([-large_sin, large_cos], axis=1),
        ],
        axis=0,
    ).astype(jnp.bfloat16)
    inputs_here = filtered.shape[1]
    spectra_here = filtered.shape[2]
    stacked = jnp.transpose(
        filtered.reshape(2, inputs_here, spectra_here, first_len, second_len), (1, 2, 0, 3, 4)
    ).reshape(inputs_here, spectra_here, 2 * first_len, second_len)
    inner = jnp.einsum("km,ismq->iskq", small_stack, stacked, preferred_element_type=jnp.float32)
    inner_real = inner[:, :, :first_len]
    inner_imag = inner[:, :, first_len:]
    turned_real = inner_real * twist_cos - inner_imag * twist_sin
    turned_imag = inner_real * twist_sin + inner_imag * twist_cos
    turned = jnp.concatenate([turned_real, turned_imag], axis=3).astype(jnp.bfloat16)
    outer = jnp.einsum("iskq,qn->isnk", turned, large_stack, preferred_element_type=jnp.float32)
    scale = NCH ** (-0.5)
    outer_real = outer[:, :, :second_len].reshape(inputs_here, spectra_here, NCH) * scale
    outer_imag = outer[:, :, second_len:].reshape(inputs_here, spectra_here, NCH) * scale
    return (outer_real, outer_imag)


def body(voltages, gains, delays, channel_order, beam_table):
    across = lax.axis_size("gx")
    along = lax.axis_size("gy")
    devices = across * along
    inputs_here = voltages.shape[1]
    width = NCH // devices
    beams_here = NBEAM // along
    frames = voltages.reshape(2, inputs_here, NSPEC + TAPS - 1, NCH)
    taps_table = coefficients()
    filtered = taps_table[0] * frames[:, :, 0:NSPEC].astype(jnp.float32)
    for tap_index in range(1, TAPS):
        filtered = filtered + taps_table[tap_index] * frames[
            :, :, tap_index : tap_index + NSPEC
        ].astype(jnp.float32)
    spec_real, spec_imag = transform(filtered.astype(jnp.bfloat16))
    gain_real = gains[0][:, None, :]
    gain_imag = gains[1][:, None, :]
    calibrated = jnp.stack(
        [
            gain_real * spec_real - gain_imag * spec_imag,
            gain_real * spec_imag + gain_imag * spec_real,
        ]
    ).astype(jnp.bfloat16)
    order = (jnp.arange(across, dtype=jnp.int32)[:, None] * along + channel_order).reshape(-1)
    blocks = jnp.take(calibrated.reshape(2, inputs_here, NSPEC, devices, width), order, axis=3)
    column = lax.axis_index("gx")
    member = lax.axis_index("gy")
    owned = column * along + channel_order[column, member]
    channel = (owned * width + jnp.arange(width, dtype=jnp.int32)).astype(jnp.float32)
    offsets = jnp.take(delays, beam_table, axis=0)
    phase = channel[:, None, None] * offsets[None] * (-2.0 * math.pi / NCH)
    scale = NIN ** (-0.5)
    weight_real = (jnp.cos(phase) * scale).astype(jnp.bfloat16)
    weight_imag = (jnp.sin(phase) * scale).astype(jnp.bfloat16)
    piece = lax.all_to_all(blocks, ("gx", "gy"), split_axis=3, concat_axis=1, tiled=True)[
        :, :, :, 0, :
    ]
    first = jnp.einsum("cbi,pisc->cbps", weight_real, piece, preferred_element_type=jnp.float32)
    second = jnp.einsum("cbi,pisc->cbps", weight_imag, piece, preferred_element_type=jnp.float32)
    beam_real = (first[:, :, 0] - second[:, :, 1]).astype(jnp.bfloat16)
    beam_imag = (first[:, :, 1] + second[:, :, 0]).astype(jnp.bfloat16)
    voltage_beams = jnp.stack([beam_real, beam_imag], axis=2)
    local_real = voltage_beams[:, :, 0].astype(jnp.float32)
    local_imag = voltage_beams[:, :, 1].astype(jnp.float32)
    local_power = (
        (local_real * local_real + local_imag * local_imag)
        .reshape(width, NBEAM, TIMES, INTEG)
        .sum(axis=3)
    )
    power = lax.all_to_all(
        local_power[None].astype(jnp.bfloat16), "gy", split_axis=2, concat_axis=0, tiled=True
    ).astype(jnp.float32)
    return jnp.transpose(power, (2, 3, 0, 1)).reshape(beams_here, TIMES, along * width)


def solution(mesh):
    return jax.shard_map(
        body,
        mesh=mesh,
        in_specs=(P(None, ("gx", "gy"), None), P(None, ("gx", "gy"), None), P(), P(), P()),
        out_specs=P("gy", None, "gx"),
        check_vma=False,
    )
```

profile of v0, /device:TPU:1, one launch (start us, length us, event | category | flops | bytes accessed | tf_op | source)
XLA Modules:
  0.0 451.2 jit_solution(18060656811732604696)
XLA Ops:
  0.0 1.9 multiply_reduce_fusion
  2.9 0.8 broadcast_add_fusion
  4.5 1.2 broadcast_divide_fusion
  5.8 10.9 %reshape.208 = bf16[2,16,15,8192]{3,2,1,0:T(8,128)(2,1)} reshape(bf16[2,16,122880]{2,1,0:T(8,128)(2,1)} %param.5) | data formatting | bytes 15728640 | tf_op jit(solution)/shard_map/reshape | solution.py:92
  16.7 26.4 %fusion.10 = bf16[16,8,2,64,128]{4,1,3,0,2:T(8,128)(2,1)S(1)} fusion(bf16[2,16,15,8192]{3,2,1,0:T(8,128)(2,1)} %reshape.208, f32[8192]{0:T(1024)S(1)} %get-tuple-element.12, f32[8192]{0:T(1024)S(1)} %get-tuple-element.13, f32[8192]{0:T(1024)S(1)} %get-tuple-element.14, f32[8192]{0:T(1024)S(1)} %get-tuple-element.15, f32[8192]{0:T(1024)S(1)} %get-tuple-element.16, ...), kind=kLoop, calls=%fused_computation.20 | loop fusion | flops 50331648 | bytes 38010880 | tf_op jit(solution)/shard_map/transpose | solution.py:69
  43.1 3.2 copy.24
  46.4 0.4 mul.511
  46.9 0.3 copy.25
  47.2 0.4 mul.515
  47.6 0.3 copy.26
  47.9 3.5 convolution_bitcast_fusion
  51.4 1.2 subtract_convert_fusion.1
  52.6 1.2 fusion.11
  53.9 1.3 fusion.14
  55.2 2.3 pad_maximum_fusion
  57.6 13.0 %copy.27 = bf16[2,16,8,128,64]{4,1,2,0,3:T(8,128)(2,1)} copy(bf16[2,16,8,128,64]{3,4,2,1,0:T(8,128)(2,1)} %pad_maximum_fusion) | data formatting | bytes 8388608 | tf_op jit(solution)/shard_map/stack | solution.py:102
  70.6 10.0 %gather_fusion.1 = bf16[128,2,16,8,64]{4,2,3,1,0:T(8,128)(2,1)} fusion(bf16[2,16,8,128,64]{4,1,2,0,3:T(8,128)(2,1)} %copy.27, s32[1024]{0:T(1024)S(1)} %pad_clamp_fusion), kind=kCustom, calls=%fused_computation.1 | custom fusion | bytes 8389120 | tf_op jit(solution)/shard_map/jit(_take)/gather | solution.py:109
  80.6 7.4 %fusion.83 = bf16[128,2,8,16,64]{4,3,2,1,0:T(8,128)(2,1)} fusion(bf16[128,2,16,8,64]{4,2,3,1,0:T(8,128)(2,1)} %gather_fusion.1, pred[128]{0:T(512)(128)(4,1)S(1)} %compare_and_fusion), kind=kLoop, calls=%fused_computation.135 | loop fusion | flops 2097152 | bytes 8388736
  88.0 14.8 %reshape.244 = bf16[128,2,8192]{2,1,0:T(2,128)(2,1)} reshape(bf16[128,2,8,16,64]{4,3,2,1,0:T(8,128)(2,1)} %fusion.83) | data formatting | bytes 8388608
  102.8 12.0 %all-to-all-start = ((bf16[128,2,8192]{2,1,0:T(2,128)(2,1)}), bf16[128,2,8192]{2,1,0:T(2,128)(2,1)}, u32[]{:S(2)}, u32[]{:S(2)}) async-start(bf16[128,2,8192]{2,1,0:T(2,128)(2,1)} %reshape.244), calls=%async_computation | async-start | bytes 8388608 | tf_op jit(solution)/shard_map/all_to_all | solution.py:119
  114.8 1.3 dynamic_slice.3
  116.8 0.8 gather_fusion
  117.7 50.6 %all-to-all-done = bf16[128,2,8192]{2,1,0:T(2,128)(2,1)} async-done(((bf16[128,2,8192]{2,1,0:T(2,128)(2,1)}), bf16[128,2,8192]{2,1,0:T(2,128)(2,1)}, u32[]{:S(2)}, u32[]{:S(2)}) %all-to-all-start) | async-done | bytes 4194336 | tf_op jit(solution)/shard_map/all_to_all | solution.py:119
  168.3 14.6 %reshape.245 = bf16[128,2,8,16,64]{4,3,2,1,0:T(8,128)(2,1)} reshape(bf16[128,2,8192]{2,1,0:T(2,128)(2,1)} %all-to-all-done) | data formatting | bytes 8388608
  182.9 10.4 %bitcast_bitcast_fusion = bf16[2,128,16,8,1,64]{5,2,3,0,1,4:T(8,128)(2,1)} fusion(bf16[128,2,8,16,64]{4,3,2,1,0:T(8,128)(2,1)} %reshape.245), kind=kLoop, calls=%fused_computation.134 | loop fusion | bytes 8388608 | tf_op jit(solution)/shard_map/all_to_all | solution.py:119
  193.2 10.9 %copy.28 = bf16[2,128,16,8,1,64]{5,3,2,1,0,4:T(8,128)(2,1)} copy(bf16[2,128,16,8,1,64]{5,2,3,0,1,4:T(8,128)(2,1)} %bitcast_bitcast_fusion) | data formatting | bytes 8388608 | tf_op jit(solution)/shard_map/all_to_all | solution.py:119
  204.1 12.0 %copy.29 = bf16[2,2048,8,64]{1,2,0,3:T(8,128)(2,1)} copy(bf16[2,2048,8,64]{3,2,1,0:T(8,128)(2,1)} %bitcast.74) | data formatting | bytes 8388608 | tf_op jit(solution)/shard_map/squeeze | solution.py:119
  216.2 112.2 %fusion.4 = f32[64,64,2,8]{1,3,2,0:T(8,128)S(1)} fusion(bf16[2,2048,8,64]{1,2,0,3:T(8,128)(2,1)} %copy.29, f32[64,2048]{1,0:T(8,128)S(1)} %broadcast_select_fusion, f32[64]{0:T(128)S(1)} %add_convert_fusion.3), kind=kOutput, calls=%fused_computation.8 | convolution fusion | flops 301989888 | bytes 4980992 | tf_op jit(solution)/shard_map/cbi,pisc->cbps/dot_general | solution.py:122
  328.4 112.3 %fusion.2 = f32[64,64,2,8]{1,3,2,0:T(8,128)S(1)} fusion(bf16[2,2048,8,64]{1,2,0,3:T(8,128)(2,1)S(1)} %copy-done.2, f32[64,2048]{1,0:T(8,128)S(1)} %broadcast_select_fusion, f32[64]{0:T(128)S(1)} %add_convert_fusion.3), kind=kOutput, calls=%fused_computation.7 | convolution fusion | flops 301989888 | bytes 4980992 | tf_op jit(solution)/shard_map/cbi,pisc->cbps/dot_general | solution.py:123
  440.8 0.4 reduce_sum.19
  441.4 8.6 %all_to_all.24 = bf16[16,2,512]{2,1,0:T(2,128)(2,1)S(1)} all-to-all(bf16[16,2,512]{2,1,0:T(2,128)(2,1)S(1)} %reshape.246), channel_id=1, replica_groups=mesh['gx'=8,'gy'=16] {'gy'}, dimensions={0} | all-to-all | bytes 65536 | tf_op jit(solution)/shard_map/all_to_all | solution.py:134
  450.1 0.7 reshape.216
  (35 shorter events, 1.9 us)
Async XLA Ops:
  0.0 116.8 %copy-start = (f32[64,2048]{1,0:T(8,128)S(1)}, f32[64,2048]{1,0:T(8,128)}, u32[]{:S(2)}) copy-start(f32[64,2048]{1,0:T(8,128)} %param.7) | copy-start | bytes 1572868
  43.1 3.2 copy-start.3
  88.0 28.7 %copy-start.4 = (s32[64]{0:T(128)S(1)}, s32[64]{0:T(128)}, u32[]{:S(2)}) copy-start(s32[64]{0:T(128)} %param.9) | copy-start | bytes 772
  102.8 65.5 %all-to-all-start = ((bf16[128,2,8192]{2,1,0:T(2,128)(2,1)}), bf16[128,2,8192]{2,1,0:T(2,128)(2,1)}, u32[]{:S(2)}, u32[]{:S(2)}) async-start(bf16[128,2,8192]{2,1,0:T(2,128)(2,1)} %reshape.244), calls=%async_computation | async-start | bytes 8388608 | tf_op jit(solution)/shard_map/all_to_all | solution.py:119
  216.2 112.2 %copy-start.2 = (bf16[2,2048,8,64]{1,2,0,3:T(8,128)(2,1)S(1)}, bf16[2,2048,8,64]{1,2,0,3:T(8,128)(2,1)}, u32[]{:S(2)}) copy-start(bf16[2,2048,8,64]{1,2,0,3:T(8,128)(2,1)} %copy.29) | copy-start | bytes 12582916
  328.4 122.5 %copy-start.1 = (f32[64,2048]{1,0:T(8,128)S(1)}, f32[64,2048]{1,0:T(8,128)}, u32[]{:S(2)}) copy-start(f32[64,2048]{1,0:T(8,128)} %param.7) | copy-start | bytes 1572868
where the time goes:
time: 460 us; the launch traced here: 451 us
  matrix products  229 us (50%)
  local copies, waits for them, and re-layouts  105 us (23%)
  waiting for transfers between devices  50.6 us (11%)
  other arithmetic  44.3 us (10%)
  starting transfers between devices  12 us (3%)
  blocking collectives  8.56 us (2%)
    dot_general x1, matrix products, body(): jnp.einsum('cbi,pisc->cbps', weight_imag, piece, preferred_element_type=j...  112 us
    dot_general x1, matrix products, body(): jnp.einsum('cbi,pisc->cbps', weight_real, piece, preferred_element_type=j...  112 us
    all_to_all x1, waiting for transfers between devices, body(): lax.all_to_all(blocks, ('gx', 'gy'), split_axis=3, concat_axis=1, tiled=T...  50.6 us
    unnamed x14, local copies, waits for them, and re-layouts  29.6 us
    transpose x1, other arithmetic, transform(): jnp.transpose(filtered.reshape(2, inputs_here, spectra_here, first_len, s...  26.4 us
    all_to_all x2, local copies, waits for them, and re-layouts, body(): lax.all_to_all(blocks, ('gx', 'gy'), split_axis=3, concat_axis=1, tiled=T...  21.2 us
    another operation x1, local copies, waits for them, and re-layouts, body(): jnp.stack([gain_real * spec_real - gain_imag * spec_imag, gain_real * spe...  13 us
    squeeze x1, local copies, waits for them, and re-layouts, body(): lax.all_to_all(blocks, ('gx', 'gy'), split_axis=3, concat_axis=1, tiled=T...  12 us
  transfers between devices with their start and end apart: 1, of which 1 were waited for; matrix products, arithmetic and copies ran while one was open for 0% of the time, Pallas kernels for 0%

commit v1 on v0

v1 whole, which is shorter than its diff:
```python
import functools
import math

import jax
import jax.numpy as jnp
import numpy as np
from jax import lax
from jax.experimental import pallas as pl
from jax.experimental.pallas import tpu as pltpu
from jax.sharding import PartitionSpec as P

NIN = 2048
NCH = 8192
NBEAM = 64
TAPS = 8
INTEG = 2
NSPEC = 8
TIMES = 4
FRAMES = NSPEC + TAPS - 1
K1 = 64
Q = 128
HERE = 16
GROUPS = 4
KK = K1 // GROUPS
PIECES = 4
PIECE = NCH // PIECES
MESH = pl.DeviceIdType.MESH
F32 = jnp.float32
BF16 = jnp.bfloat16


def tables():
    n = np.arange(TAPS * NCH, dtype=np.float64)
    raw = np.sinc((n - TAPS * NCH / 2) / NCH) * (0.5 - 0.5 * np.cos(2 * np.pi * n / (TAPS * NCH)))
    coef = (raw / np.sqrt(np.sum(raw * raw) / NCH)).reshape(TAPS, NCH).astype(np.float32)
    k = np.arange(K1)
    q = np.arange(Q)
    ang = 2 * np.pi / K1 * (k[:, None] * k[None, :] % K1)
    c, s = np.cos(ang), np.sin(ang)
    first = np.block([[c, s], [-s, c]]).astype(np.float32)
    ang = 2 * np.pi / NCH * (k[:, None] * q[None, :])
    twist = np.stack([np.cos(ang), -np.sin(ang)]).astype(np.float32)
    ang = 2 * np.pi / Q * (q[:, None] * q[None, :] % Q)
    c, s = np.cos(ang), np.sin(ang)
    second = np.concatenate([c, s, -s, c], axis=1).astype(np.float32)
    col = np.arange(GROUPS * NSPEC * KK)
    chan = col // (NSPEC * KK) * KK + col % KK
    row = np.arange(256) % K1
    spread = (row[:, None] == chan[None, :]).astype(np.float32)
    return (
        jnp.asarray(coef),
        jnp.asarray(first, dtype=BF16),
        jnp.asarray(twist),
        jnp.asarray(second, dtype=BF16),
        jnp.asarray(spread, dtype=BF16),
    )


def times(a, b):
    return a[0] * b[0] - a[1] * b[1], a[0] * b[1] + a[1] * b[0]


def kernel(
    volt,
    gains_hbm,
    order,
    offsets,
    coef,
    first,
    twist,
    second,
    spread,
    out,
    gains,
    gcol,
    gsel,
    turned,
    stage,
    send,
    recv,
    power,
    landed,
    gain_sem,
    send_sem,
    recv_sem,
    psend_sem,
    precv_sem,
):
    gx = lax.axis_index("gx")
    gy = lax.axis_index("gy")
    me = gx * 16 + gy
    mx, my, mz, mc = gx // 2, (gx % 2) * 2 + (gy // 2) % 2, gy // 4, gy % 2

    barrier = pltpu.get_barrier_semaphore()

    def greet(j, carry):
        d = lax.rem(me + j, Q)
        pl.semaphore_signal(barrier, inc=1, device_id=(d // 16, d % 16), device_id_type=MESH)
        return carry

    gains_copy = pltpu.make_async_copy(gains_hbm, gains, gain_sem)

    def filterbank(frames, filt, frame_sem):
        for c in range(PIECES):
            for f in range(FRAMES):
                pltpu.make_async_copy(
                    volt.at[:, :, pl.ds(f * NCH + c * PIECE, PIECE)], frames.at[c, f], frame_sem.at[c]
                ).start()
        gains_copy.start()
        lax.fori_loop(1, Q, greet, 0)

        for c in range(PIECES):
            pltpu.make_async_copy(frames.at[c], frames.at[c], frame_sem.at[c]).wait()

            def fir(a, carry, c=c):
                here = pl.ds(pl.multiple_of(a * Q, Q), Q)
                there = pl.ds(pl.multiple_of(c * PIECE + a * Q, Q), Q)
                taps = [jnp.broadcast_to(coef[pl.ds(t, 1), there], (HERE, Q)) for t in range(TAPS)]
                for p in range(2):
                    x = [frames[c, f, p, :, here].astype(F32) for f in range(FRAMES)]
                    for s in range(NSPEC):
                        acc = taps[0] * x[s]
                        for t in range(1, TAPS):
                            acc = acc + taps[t] * x[s + t]
                        row = s * HERE * Q + p * K1 + c * (PIECE // Q) + a
                        filt[pl.ds(row, HERE, stride=Q), :] = acc
                return carry

            lax.fori_loop(0, PIECE // Q, fir, 0)

        def dft1(i, carry):
            x = [filt[pl.ds(pl.multiple_of((s * HERE + i) * Q, Q), Q), :].astype(BF16) for s in range(NSPEC)]
            x = jnp.concatenate(x, axis=1)
            inner = jnp.dot(first[...], x, preferred_element_type=F32)
            tc, ts = twist[0], twist[1]
            for s in range(NSPEC):
                re = inner[:K1, s * Q : (s + 1) * Q]
                im = inner[K1:, s * Q : (s + 1) * Q]
                tre = (re * tc - im * ts).astype(BF16)
                tim = (re * ts + im * tc).astype(BF16)
                for g in range(GROUPS):
                    rows = pl.ds(pl.multiple_of(i * Q + s * KK, KK), KK)
                    turned[g, rows, 0:Q] = tre[g * KK : (g + 1) * KK]
                    turned[g, rows, Q : 2 * Q] = tim[g * KK : (g + 1) * KK]
            return carry

        lax.fori_loop(0, HERE, dft1, 0)

    pl.run_scoped(
        filterbank,
        pltpu.VMEM((PIECES, FRAMES, 2, HERE, PIECE), BF16),
        pltpu.VMEM((NSPEC * HERE * Q, Q), F32),
        pltpu.SemaphoreType.DMA((PIECES,)),
    )

    gains_copy.wait()
    for j in range(NCH // Q):
        for p in range(2):
            gcol[pl.ds(p * HERE * K1 + j, HERE, stride=K1), :] = gains[p, :, j * Q : (j + 1) * Q]
    lane = lax.broadcasted_iota(jnp.int32, (Q, Q), 1)
    owner = order[...]
    one_hot = (owner == lane).astype(F32).astype(BF16)
    half_hot = ((owner // 2) == lane).astype(F32).astype(BF16)[:, :K1]
    parity = ((owner % 2) == lane // K1).astype(F32)
    parity = jnp.concatenate([parity, parity], axis=1)
    table = jnp.dot(one_hot, second[...], preferred_element_type=F32).astype(BF16)
    table = jnp.concatenate([table[:, : 2 * Q], table[:, 2 * Q :]], axis=0)

    def pick(i, carry):
        for p in range(2):
            g = gcol[pl.ds(pl.multiple_of((p * HERE + i) * K1, K1), K1), :] * F32(NCH**-0.5)
            hi = g.astype(BF16)
            lo = (g - hi.astype(F32)).astype(BF16)
            both = jnp.dot(half_hot, jnp.concatenate([hi, lo], axis=1), preferred_element_type=F32)
            gsel[pl.ds(pl.multiple_of(i * 2 * Q + p * Q, Q), Q), :] = (both * parity).astype(BF16)
        return carry

    lax.fori_loop(0, HERE, pick, 0)

    pl.semaphore_wait(barrier, Q - 1)

    for g in range(GROUPS):
        cols = slice(g * 2 * Q, (g + 1) * 2 * Q)

        def dft2(ii, carry, g=g):
            x = turned[g, pl.ds(pl.multiple_of(ii * 2 * Q, 2 * Q), 2 * Q), :]
            spec = lax.dot_general(table, x, (((1,), (1,)), ((), ())), preferred_element_type=F32)
            gain = jnp.dot(
                gsel[pl.ds(pl.multiple_of(ii * 4 * Q, 4 * Q), 4 * Q), :],
                spread[:, g * Q : (g + 1) * Q],
                preferred_element_type=F32,
            )
            for u in range(2):
                gr = gain[u * 2 * Q : u * 2 * Q + Q]
                gi = gain[u * 2 * Q + Q : (u + 1) * 2 * Q]
                sr = spec[:Q, u * Q : (u + 1) * Q]
                si = spec[Q:, u * Q : (u + 1) * Q]
                stage[pl.ds(ii * 2 + u, Q, stride=HERE), :] = gr * sr - gi * si
                stage[pl.ds(Q * HERE + ii * 2 + u, Q, stride=HERE), :] = gr * si + gi * sr
            return carry

        lax.fori_loop(0, HERE // 2, dft2, 0)

        def cast(r, carry, g=g):
            for p in range(2):
                rows = pl.ds(pl.multiple_of(r * Q, Q), Q)
                x = stage[pl.ds(pl.multiple_of(p * Q * HERE + r * Q, Q), Q), :]
                send[rows, (g * 2 + p) * Q : (g * 2 + p + 1) * Q] = x.astype(BF16)
            return carry

        lax.fori_loop(0, HERE, cast, 0)
        mine = pl.ds(pl.multiple_of(me * HERE, HERE), HERE)

        def hand_out(j, carry, g=g, cols=cols, mine=mine):
            jj = j // 2
            dx = jj % 4
            dy = (jj // 4 + dx) % 4
            dz = (jj // 16 + dy + mc * 2) % 4
            x, y, z, core = (mx + dx) % 4, (my + dy) % 4, (mz + dz) % 4, (mc + j % 2) % 2
            da = x * 2 + y // 2
            db = (z * 2 + y % 2) * 2 + core
            d = da * 16 + db

            @pl.when(d != me)
            def _():
                pltpu.make_async_remote_copy(
                    src_ref=send.at[pl.ds(pl.multiple_of(d * HERE, HERE), HERE), cols],
                    dst_ref=recv.at[mine, cols],
                    send_sem=send_sem.at[g],
                    recv_sem=recv_sem.at[g],
                    device_id=(da, db),
                    device_id_type=MESH,
                ).start()

            return carry

        lax.fori_loop(0, Q, hand_out, 0)
        recv[mine, cols] = send[mine, cols]

    def beamform(weights):
        centre = order[pl.ds(me, 1), :].astype(F32) * K1 + (K1 - 1) / 2

        def weigh(n, carry):
            lanes = pl.ds(pl.multiple_of(n // 4 * Q, Q), Q)
            r0 = n % 4 * 16
            step = offsets[pl.ds(pl.multiple_of(r0, 16), 16), lanes]
            phase = (step * centre) * F32(2 * math.pi / NCH)
            scale = F32(NIN**-0.5)
            mid = (jnp.cos(phase) * scale, -jnp.sin(phase) * scale)
            half = step * F32(math.pi / NCH)
            z1 = (jnp.cos(half), -jnp.sin(half))
            z2 = times(z1, z1)
            z3 = times(z2, z1)
            z5 = times(z3, z2)
            z7 = times(z5, z2)
            z8 = times(z7, z1)
            z16 = times(z8, z8)
            z24 = times(z16, z8)
            z40 = times(z24, z16)
            z56 = times(z40, z16)

            def both(a, b):
                rr, ii, ri, ir = a[0] * b[0], a[1] * b[1], a[0] * b[1], a[1] * b[0]
                return (rr - ii, ir + ri), (rr + ii, ir - ri)

            for far, zf in ((8, z8), (24, z24), (40, z40), (56, z56)):
                for sf, anchor in zip((1, -1), both(mid, zf)):
                    for near, zn in ((1, z1), (3, z3), (5, z5), (7, z7)):
                        for sn, w in zip((1, -1), both(anchor, zn)):
                            k = (K1 - 1 + sf * far + sn * near) // 2
                            for ri in range(2):
                                row = (k * 2 + ri) * NBEAM + r0
                                weights[pl.ds(pl.multiple_of(row, 16), 16), lanes] = w[ri].astype(BF16)
            return carry

        lax.fori_loop(0, NIN // Q * 4, weigh, 0)

        lane = lax.broadcasted_iota(jnp.int32, (Q, 2 * Q), 1) % KK
        srow = lax.broadcasted_iota(jnp.int32, (Q, Q), 0)
        scol = lax.broadcasted_iota(jnp.int32, (Q, Q), 1)
        made = None
        for g in range(GROUPS):
            cols = slice(g * 2 * Q, (g + 1) * 2 * Q)
            arrived = recv.at[pl.ds(0, (Q - 1) * HERE), cols]
            pltpu.make_async_copy(arrived, arrived, recv_sem.at[g]).wait()

            def form(m, acc, g=g, cols=cols):
                rows = pl.ds(pl.multiple_of(g * KK * Q + m * 4 * Q, 4 * Q), 4 * Q)
                res = jnp.dot(weights[rows, :], recv[:, cols], preferred_element_type=F32)
                for u in range(4):
                    acc = jnp.where(lane == m * 4 + u, res[u * Q : (u + 1) * Q], acc)
                return acc

            acc = lax.fori_loop(0, KK // 4, form, jnp.zeros((Q, 2 * Q), F32))
            br = (acc[:NBEAM, :Q] - acc[NBEAM:, Q:]).astype(BF16).astype(F32)
            bi = (acc[:NBEAM, Q:] + acc[NBEAM:, :Q]).astype(BF16).astype(F32)
            pw = br * br + bi * bi
            target = g % 2 * K1 + srow // (2 * KK) * KK + srow % KK
            gather = (target == scol).astype(F32)
            part = jnp.dot(pw, gather, preferred_element_type=F32, precision=lax.Precision.HIGHEST)
            made = part if g % 2 == 0 else made + part
            if g % 2:
                for b in range(16):
                    power[b * 8 + g // 2 * 4 : b * 8 + g // 2 * 4 + 4, :] = made[b * 4 : b * 4 + 4]

    pl.run_scoped(beamform, pltpu.VMEM((K1 * 2 * NBEAM, NIN), BF16))

    spot = pl.ds(pl.multiple_of(gy * 8, 8), 8)

    def deliver(j, carry):
        b = lax.rem(gy + j, 16)
        pltpu.make_async_remote_copy(
            src_ref=power.at[pl.ds(pl.multiple_of(b * 8, 8), 8), :],
            dst_ref=landed.at[spot, :],
            send_sem=psend_sem,
            recv_sem=precv_sem,
            device_id=(gx, b),
            device_id_type=MESH,
        ).start()
        return carry

    lax.fori_loop(1, 16, deliver, 0)
    landed[spot, :] = power[spot, :]
    for g in range(GROUPS):
        sent = send.at[pl.ds(0, (Q - 1) * HERE), pl.ds(g * 2 * Q, 2 * Q)]
        pltpu.make_async_copy(sent, sent, send_sem.at[g]).wait()
    pltpu.make_async_copy(power.at[0:120], power.at[0:120], psend_sem).wait()
    pltpu.make_async_copy(landed.at[0:120], landed.at[0:120], precv_sem).wait()
    out[...] = landed[...]


def body(voltages, gains, delays, channel_order, beam_table):
    along = lax.axis_size("gy")
    order = (jnp.arange(lax.axis_size("gx"), dtype=jnp.int32)[:, None] * along + channel_order).reshape(-1)
    order = jnp.broadcast_to(order[:, None], (Q, Q))
    offsets = jnp.take(delays, beam_table, axis=0)
    vmem = pl.BlockSpec(memory_space=pltpu.VMEM)
    hbm = pl.BlockSpec(memory_space=pl.ANY)
    landed = pl.pallas_call(
        kernel,
        out_shape=jax.ShapeDtypeStruct((Q, Q), F32),
        in_specs=[hbm, hbm] + [vmem] * 7,
        out_specs=vmem,
        scratch_shapes=[
            pltpu.VMEM((2, HERE, NCH), F32),
            pltpu.VMEM((2 * HERE * K1, Q), F32),
            pltpu.VMEM((HERE * 2 * Q, 2 * Q), BF16),
            pltpu.VMEM((GROUPS, HERE * Q, 2 * Q), BF16),
            pltpu.VMEM((2 * HERE * Q, Q), F32),
            pltpu.VMEM((Q * HERE, GROUPS * 2 * Q), BF16),
            pltpu.VMEM((Q * HERE, GROUPS * 2 * Q), BF16),
            pltpu.VMEM((Q, Q), F32),
            pltpu.VMEM((Q, Q), F32),
            pltpu.SemaphoreType.DMA,
            pltpu.SemaphoreType.DMA((GROUPS,)),
            pltpu.SemaphoreType.DMA((GROUPS,)),
            pltpu.SemaphoreType.DMA,
            pltpu.SemaphoreType.DMA,
        ],
        compiler_params=pltpu.CompilerParams(
            collective_id=0, has_side_effects=True, vmem_limit_bytes=60 * 2**20
        ),
    )(voltages, gains, order, offsets, *tables())
    landed = landed.reshape(16, 2, 4, 2, TIMES, KK)
    return jnp.transpose(landed, (2, 4, 0, 1, 3, 5)).reshape(NBEAM // along, TIMES, along * K1)


def solution(mesh):
    return jax.shard_map(
        body,
        mesh=mesh,
        in_specs=(P(None, ("gx", "gy"), None), P(None, ("gx", "gy"), None), P(), P(), P()),
        out_specs=P("gy", None, "gx"),
        check_vma=False,
    )
```

time: 460 us -> 110 us (0.24); the launches traced: 451 us -> 109 us
  matrix products: 229 us -> 0 us
  Pallas kernels: 0 us -> 102 us
  local copies, waits for them, and re-layouts: 105 us -> 4.38 us
  waiting for transfers between devices: 50.6 us -> 0 us
  other arithmetic: 44.3 us -> 3.03 us
  starting transfers between devices: 12 us -> 0 us
  blocking collectives: 8.56 us -> 0 us
    dot_general x4 -> x0, matrix products: 229 us -> none  [the longest x1 112 us: body(): jnp.einsum('cbi,pisc->cbps', weight_imag, piece, preferred_element_type=j...]
    pallas_call x0 -> x1, Pallas kernels: none -> 102 us  [body(): pl.pallas_call(kernel, out_shape=jax.ShapeDtypeStruct((Q, Q), F32), in_sp...]
    all_to_all x1 -> x0, waiting for transfers between devices: 50.6 us -> none  [body(): lax.all_to_all(blocks, ('gx', 'gy'), split_axis=3, concat_axis=1, tiled=T...]
    unnamed x14 -> x2, local copies, waits for them, and re-layouts: 29.6 us -> 0.01 us
    transpose x1 -> x0, other arithmetic: 26.4 us -> none  [transform(): jnp.transpose(filtered.reshape(2, inputs_here, spectra_here, first_len, s...]
    all_to_all x3 -> x0, local copies, waits for them, and re-layouts: 21.3 us -> none  [the longest x2 21.2 us: body(): lax.all_to_all(blocks, ('gx', 'gy'), split_axis=3, concat_axis=1, tiled=T...]
    another operation x1 -> x0, local copies, waits for them, and re-layouts: 13 us -> none  [body(): jnp.stack([gain_real * spec_real - gain_imag * spec_imag, gain_real * spe...]
    squeeze x1 -> x0, local copies, waits for them, and re-layouts: 12 us -> none  [body(): lax.all_to_all(blocks, ('gx', 'gy'), split_axis=3, concat_axis=1, tiled=T...]
  transfers between devices with their start and end apart: 1 -> 0, of which waited for: 1 -> 0; matrix products, arithmetic and copies ran while one was open for 0% -> 0% of each run, Pallas kernels for 0% -> 0%
where the time goes in v1:
time: 110 us; the launch traced here: 109 us
  Pallas kernels  102 us (93%)
  local copies, waits for them, and re-layouts  4.38 us (4%)
  other arithmetic  3.03 us (3%)
    pallas_call x1, Pallas kernels, body(): pl.pallas_call(kernel, out_shape=jax.ShapeDtypeStruct((Q, Q), F32), in_sp...  102 us

profile of v1, /device:TPU:1, one launch (start us, length us, event | category | flops | bytes accessed | tf_op | source)
XLA Modules:
  0.0 109.4 jit_solution(18123729783350830365)
XLA Ops:
  0.0 0.0 copy-start
  0.0 0.7 compare_and_fusion
  0.7 0.7 compare_select_fusion
  1.4 0.8 broadcast_add_fusion
  2.1 0.1 broadcast_in_dim.20
  2.2 0.7 broadcast_in_dim.21.order
  2.9 0.0 copy-done
  2.9 0.8 gather_fusion
  3.7 0.9 broadcast_select_fusion.offsets
  4.6 102.0 %shard_map.100 = f32[128,128]{1,0:T(8,128)} custom-call(bf16[2,16,122880]{2,1,0:T(8,128)(2,1)} %volt.1, f32[2,16,8192]{2,1,0:T(8,128)} %gains_hbm.1, s32[128,128]{1,0:T(8,128)} %broadcast_in_dim.21.order, f32[64,2048]{1,0:T(8,128)} %broadcast_select_fusion.offsets, f32[8,8192]{1,0:T(8,128)} %constant.28.clone.coef, bf16[128,128]{1,0:T(8,128)(2,1)} %constant.29.clone.first, ...), custom_call_target="tpu_custom_call" | custom-call | tf_op jit(solution)/shard_map/pallas_call | solution.py:339
  106.6 1.2 %reshape.17 = f32[16,2,4,2,4,16]{5,4,3,2,1,0:T(4,128)S(1)} reshape(f32[128,128]{1,0:T(8,128)} %shard_map.100) | data formatting | bytes 131072 | tf_op jit(solution)/shard_map/reshape | solution.py:364
  107.8 0.3 copy.11
  108.1 1.3 %reshape.18 = f32[4,4,1024]{2,1,0:T(4,128)} reshape(f32[4,4,16,2,2,16]{5,4,3,2,1,0:T(2,128)S(1)} %copy.11) | data formatting | bytes 131072 | tf_op jit(solution)/shard_map/reshape | solution.py:365
  (2 shorter events, 0.0 us)
Async XLA Ops:
  0.0 2.9 %copy-start = (f32[64,2048]{1,0:T(8,128)S(1)}, f32[64,2048]{1,0:T(8,128)}, u32[]{:S(2)}) copy-start(f32[64,2048]{1,0:T(8,128)} %param.12) | copy-start | bytes 1572868

commit v2 on v1

v2 whole, which is shorter than its diff:
```python
import functools
import math

import jax
import jax.numpy as jnp
import numpy as np
from jax import lax
from jax.experimental import pallas as pl
from jax.experimental.pallas import tpu as pltpu
from jax.sharding import PartitionSpec as P

NIN = 2048
NCH = 8192
NBEAM = 64
TAPS = 8
INTEG = 2
NSPEC = 8
TIMES = 4
FRAMES = NSPEC + TAPS - 1
K1 = 64
QP = 136
HP = 24
KP = 72
Q = 128
HERE = 16
GROUPS = 4
KK = K1 // GROUPS
EARLY = 32
LATE = 2
PIECES = 4
PIECE = NCH // PIECES
MESH = pl.DeviceIdType.MESH
F32 = jnp.float32
BF16 = jnp.bfloat16


def tables():
    n = np.arange(TAPS * NCH, dtype=np.float64)
    raw = np.sinc((n - TAPS * NCH / 2) / NCH) * (0.5 - 0.5 * np.cos(2 * np.pi * n / (TAPS * NCH)))
    coef = (raw / np.sqrt(np.sum(raw * raw) / NCH)).reshape(TAPS, NCH).astype(np.float32)
    k = np.arange(K1)
    q = np.arange(Q)
    ang = 2 * np.pi / K1 * (k[:, None] * k[None, :] % K1)
    c, s = np.cos(ang), np.sin(ang)
    first = np.block([[c, s], [-s, c]]).astype(np.float32)
    ang = 2 * np.pi / NCH * (k[:, None] * q[None, :])
    twist = np.stack([np.cos(ang), -np.sin(ang)]).astype(np.float32)
    ang = 2 * np.pi / Q * (q[:, None] * q[None, :] % Q)
    c, s = np.cos(ang), np.sin(ang)
    second = np.concatenate([c, s, -s, c], axis=1).astype(np.float32)
    col = np.arange(GROUPS * NSPEC * KK)
    chan = col // (NSPEC * KK) * KK + col % KK
    row = np.arange(256) % K1
    spread = (row[:, None] == chan[None, :]).astype(np.float32)
    return (
        jnp.asarray(coef),
        jnp.asarray(first, dtype=BF16),
        jnp.asarray(twist),
        jnp.asarray(second, dtype=BF16),
        jnp.asarray(spread, dtype=BF16),
    )


def times(a, b):
    return a[0] * b[0] - a[1] * b[1], a[0] * b[1] + a[1] * b[0]


def eighth(x):
    y = x * x
    c = 1 + y * (-1 / 2 + y * (1 / 24 + y * (-1 / 720 + y * (1 / 40320))))
    s = x + x * y * (-1 / 6 + y * (1 / 120 + y * (-1 / 5040 + y * (1 / 362880))))
    return c, s


def kernel(
    volt,
    gains_hbm,
    channel_order,
    beam_table,
    delays,
    coef,
    first,
    twist,
    second,
    spread,
    out,
    gains,
    order,
    offsets,
    gcol,
    gsel,
    turned,
    stage,
    send,
    recv,
    power,
    landed,
    target,
    gain_sem,
    send_sem,
    recv_sem,
    psend_sem,
    precv_sem,
):
    gx = lax.axis_index("gx")
    gy = lax.axis_index("gy")
    me = gx * 16 + gy
    mx, my, mz, mc = gx // 2, (gx % 2) * 2 + (gy // 2) % 2, gy // 4, gy % 2

    barrier = pltpu.get_barrier_semaphore()

    def greet(a, carry):
        for b in range(16):
            pl.semaphore_signal(barrier, inc=1, device_id=(lax.rem(gx + a, 8), b), device_id_type=MESH)
        return carry

    def plan(m, carry):
        a, b = lax.div(m, 4), lax.rem(m, 4)
        for dx in range(4):
            x = lax.rem(mx + dx, 4)
            dy = lax.rem(b + dx, 4)
            y = lax.rem(my + dy, 4)
            z = lax.rem(mz + a + dy, 4)
            da = x * 2 + lax.div(y, 2)
            db = (z * 2 + lax.rem(y, 2)) * 2
            for core in range(2):
                target[0, m * 8 + dx * 2 + core] = da
                target[1, m * 8 + dx * 2 + core] = db + lax.rem(mc + core, 2)
        return carry

    gains_copy = pltpu.make_async_copy(gains_hbm, gains, gain_sem)

    def filterbank(frames, filt, frame_sem):
        gains_copy.start()
        for c in range(PIECES):
            for f in range(FRAMES):
                pltpu.make_async_copy(
                    volt.at[:, :, pl.ds(f * NCH + c * PIECE, PIECE)], frames.at[c, f], frame_sem.at[c]
                ).start()
        lax.fori_loop(1, 8, greet, 0)
        for b in range(1, 16):
            pl.semaphore_signal(barrier, inc=1, device_id=(gx, lax.rem(gy + b, 16)), device_id_type=MESH)
        lax.fori_loop(0, 16, plan, 0)
        owned = [jnp.broadcast_to(channel_order[a : a + 1, :], (16, 16)).astype(F32) + a * 16 for a in range(8)]
        owned = jnp.concatenate(owned, axis=0)
        row = lax.broadcasted_iota(jnp.int32, (Q, 16), 0) % 16
        col = lax.broadcasted_iota(jnp.int32, (Q, 16), 1)
        owned = jnp.sum(jnp.where(row == col, owned, 0.0), axis=1, keepdims=True)
        order[...] = jnp.broadcast_to(owned, (Q, Q)).astype(jnp.int32)

        for c in range(PIECES):
            pltpu.make_async_copy(frames.at[c], frames.at[c], frame_sem.at[c]).wait()

            def fir(a, carry, c=c):
                here = pl.ds(pl.multiple_of(a * Q, Q), Q)
                there = pl.ds(pl.multiple_of(c * PIECE + a * Q, Q), Q)
                taps = [jnp.broadcast_to(coef[pl.ds(t, 1), there], (HERE, Q)) for t in range(TAPS)]
                for p in range(2):
                    x = [frames[c, f, p, :, here].astype(F32) for f in range(FRAMES)]
                    for s in range(NSPEC):
                        acc = taps[0] * x[s]
                        for t in range(1, TAPS):
                            acc = acc + taps[t] * x[s + t]
                        row = s * HERE * QP + p * K1 + c * (PIECE // Q) + a
                        filt[pl.ds(row, HERE, stride=QP), :] = acc
                return carry

            lax.fori_loop(0, PIECE // Q, fir, 0)

        def dft1(n, carry):
            tc, ts = twist[0], twist[1]
            for i in (n * 2, n * 2 + 1):
                for s2 in range(0, NSPEC, 2):
                    x = [
                        filt[pl.ds(pl.multiple_of((s * HERE + i) * QP, 8), Q), :].astype(BF16)
                        for s in (s2, s2 + 1)
                    ]
                    inner = jnp.dot(first[...], jnp.concatenate(x, axis=1), preferred_element_type=F32)
                    for s in range(2):
                        re = inner[:K1, s * Q : (s + 1) * Q]
                        im = inner[K1:, s * Q : (s + 1) * Q]
                        tre = (re * tc - im * ts).astype(BF16)
                        tim = (re * ts + im * tc).astype(BF16)
                        for g in range(GROUPS):
                            rows = pl.ds(pl.multiple_of(i * Q + (s2 + s) * KK, KK), KK)
                            turned[g, rows, 0:Q] = tre[g * KK : (g + 1) * KK]
                            turned[g, rows, Q : 2 * Q] = tim[g * KK : (g + 1) * KK]
            return carry

        lax.fori_loop(0, HERE // 2, dft1, 0)

    pl.run_scoped(
        filterbank,
        pltpu.VMEM((PIECES, FRAMES, 2, HERE, PIECE), BF16),
        pltpu.VMEM((NSPEC * HERE * QP, Q), F32),
        pltpu.SemaphoreType.DMA((PIECES,)),
    )

    gains_copy.wait()
    for j in range(NCH // Q):
        for p in range(2):
            gcol[pl.ds(p * HERE * KP + j, HERE, stride=KP), :] = gains[p, :, j * Q : (j + 1) * Q]
    lane = lax.broadcasted_iota(jnp.int32, (Q, Q), 1)
    owner = order[...]
    one_hot = (owner == lane).astype(F32).astype(BF16)
    half_hot = ((owner // 2) == lane).astype(F32).astype(BF16)[:, :K1]
    parity = ((owner % 2) == lane // K1).astype(F32)
    parity = jnp.concatenate([parity, parity], axis=1)
    table = jnp.dot(one_hot, second[...], preferred_element_type=F32).astype(BF16)
    table = jnp.concatenate([table[:, : 2 * Q], table[:, 2 * Q :]], axis=0)

    def pick(n, carry):
        for i in range(4):
            for p in range(2):
                at = pl.multiple_of((p * HERE + n * 4 + i) * KP, 8)
                g = gcol[pl.ds(at, K1), :] * F32(NCH**-0.5)
                hi = g.astype(BF16)
                lo = (g - hi.astype(F32)).astype(BF16)
                both = jnp.dot(half_hot, jnp.concatenate([hi, lo], axis=1), preferred_element_type=F32)
                at = pl.multiple_of((n * 4 + i) * 2 * Q + p * Q, Q)
                gsel[pl.ds(at, Q), :] = (both * parity).astype(BF16)
        return carry

    lax.fori_loop(0, HERE // 4, pick, 0)

    pl.semaphore_wait(barrier, Q - 1)

    mine = pl.ds(pl.multiple_of(me * HERE, HERE), HERE)

    def hand_out(g, j):
        da, db = target[0, j], target[1, j]
        cols = pl.ds(pl.multiple_of(g * 2 * Q, 2 * Q), 2 * Q)
        pltpu.make_async_remote_copy(
            src_ref=send.at[pl.ds(pl.multiple_of((da * 16 + db) * HERE, HERE), HERE), cols],
            dst_ref=recv.at[mine, cols],
            send_sem=send_sem.at[g],
            recv_sem=recv_sem.at[g],
            device_id=(da, db),
            device_id_type=MESH,
        ).start()

    def hand_out_many(g, start, count):
        def one(j, carry):
            hand_out(g, j)
            return carry

        lax.fori_loop(jnp.maximum(start, 1), start + count, one, 0)

    for g in range(GROUPS):
        cols = slice(g * 2 * Q, (g + 1) * 2 * Q)

        def dft2(ii, carry, g=g):
            if g:
                hand_out_many(g - 1, ii * EARLY, EARLY)
            for v in range(2):
                at = ii * 2 + v
                x = turned[g, pl.ds(pl.multiple_of(at * 2 * Q, 2 * Q), 2 * Q), :]
                spec = lax.dot_general(table, x, (((1,), (1,)), ((), ())), preferred_element_type=F32)
                gain = jnp.dot(
                    gsel[pl.ds(pl.multiple_of(at * 4 * Q, 4 * Q), 4 * Q), :],
                    spread[:, g * Q : (g + 1) * Q],
                    preferred_element_type=F32,
                )
                for u in range(2):
                    gr = gain[u * 2 * Q : u * 2 * Q + Q]
                    gi = gain[u * 2 * Q + Q : (u + 1) * 2 * Q]
                    sr = spec[:Q, u * Q : (u + 1) * Q]
                    si = spec[Q:, u * Q : (u + 1) * Q]
                    stage[pl.ds(at * 2 + u, Q, stride=HP), :] = gr * sr - gi * si
                    stage[pl.ds(Q * HP + at * 2 + u, Q, stride=HP), :] = gr * si + gi * sr
            return carry

        lax.fori_loop(0, HERE // 4, dft2, 0)

        def cast(r, carry, g=g):
            for p in range(2):
                for w in range(8):
                    rows = pl.ds(pl.multiple_of(r * Q + w * HERE, HERE), HERE)
                    x = stage[pl.ds(pl.multiple_of(p * Q * HP + (r * 8 + w) * HP, 8), HERE), :]
                    send[rows, (g * 2 + p) * Q : (g * 2 + p + 1) * Q] = x.astype(BF16)
            return carry

        lax.fori_loop(0, HERE, cast, 0)
        recv[mine, cols] = send[mine, cols]

    def beamform(weights):
        centre = order[pl.ds(me, 1), :].astype(F32) * K1 + (K1 - 1) / 2

        def beam(r, carry):
            offsets[pl.ds(r, 1), :] = delays[pl.ds(beam_table[r], 1), :]
            return carry

        lax.fori_loop(0, NBEAM, beam, 0)

        def weigh(n, carry):
            hand_out_many(GROUPS - 1, n * LATE, LATE)
            lanes = pl.ds(pl.multiple_of(n // 4 * Q, Q), Q)
            r0 = n % 4 * 16
            step = offsets[pl.ds(pl.multiple_of(r0, 16), 16), lanes]
            turns = step * centre * F32(1 / NCH)
            mid = eighth((turns - jnp.round(turns)) * F32(-2 * math.pi / 8))
            mid = times(mid, mid)
            mid = times(mid, mid)
            mid = times(mid, mid)
            mid = (mid[0] * F32(NIN**-0.5), mid[1] * F32(NIN**-0.5))
            z1 = eighth(step * F32(-math.pi / NCH))
            z2 = times(z1, z1)
            z3 = times(z2, z1)
            z5 = times(z3, z2)
            z7 = times(z5, z2)
            z8 = times(z7, z1)
            z16 = times(z8, z8)
            z24 = times(z16, z8)
            z40 = times(z24, z16)
            z56 = times(z40, z16)

            def both(a, b):
                rr, ii, ri, ir = a[0] * b[0], a[1] * b[1], a[0] * b[1], a[1] * b[0]
                return (rr - ii, ir + ri), (rr + ii, ir - ri)

            for far, zf in ((8, z8), (24, z24), (40, z40), (56, z56)):
                for sf, anchor in zip((1, -1), both(mid, zf)):
                    for near, zn in ((1, z1), (3, z3), (5, z5), (7, z7)):
                        for sn, w in zip((1, -1), both(anchor, zn)):
                            k = (K1 - 1 + sf * far + sn * near) // 2
                            for ri in range(2):
                                row = (k * 2 + ri) * NBEAM + r0
                                weights[pl.ds(pl.multiple_of(row, 16), 16), lanes] = w[ri].astype(BF16)
            return carry

        lax.fori_loop(0, NIN // Q * 4, weigh, 0)

        lane = lax.broadcasted_iota(jnp.int32, (Q, 2 * Q), 1) % KK
        srow = lax.broadcasted_iota(jnp.int32, (Q, TIMES * Q), 0)
        scol = lax.broadcasted_iota(jnp.int32, (Q, TIMES * Q), 1)
        same_time = srow // (INTEG * KK) == scol // Q
        made = jnp.zeros((NBEAM, TIMES * Q), F32)
        for g in range(GROUPS):
            cols = slice(g * 2 * Q, (g + 1) * 2 * Q)
            arrived = recv.at[pl.ds(0, (Q - 1) * HERE), cols]
            pltpu.make_async_copy(arrived, arrived, recv_sem.at[g]).wait()

            def form(m, acc, g=g, cols=cols):
                rows = pl.ds(pl.multiple_of(g * KK * Q + m * 8 * Q, 8 * Q), 8 * Q)
                res = jnp.dot(weights[rows, :], recv[:, cols], preferred_element_type=F32)
                for u in range(8):
                    acc = jnp.where(lane == m * 8 + u, res[u * Q : (u + 1) * Q], acc)
                return acc

            acc = lax.fori_loop(0, KK // 8, form, jnp.zeros((Q, 2 * Q), F32))
            br = (acc[:NBEAM, :Q] - acc[NBEAM:, Q:]).astype(BF16).astype(F32)
            bi = (acc[:NBEAM, Q:] + acc[NBEAM:, :Q]).astype(BF16).astype(F32)
            pw = br * br + bi * bi
            gather = (same_time & (srow % KK + g * KK == scol % K1)).astype(F32)
            made += jnp.dot(pw, gather, preferred_element_type=F32, precision=lax.Precision.HIGHEST)
        for t in range(TIMES):
            power[pl.ds(t, NBEAM, stride=TIMES), :] = made[:, t * Q : (t + 1) * Q]

    pl.run_scoped(beamform, pltpu.VMEM((K1 * 2 * NBEAM, NIN), BF16))

    spot = pl.ds(pl.multiple_of(gy * 16, 16), 16)

    def deliver(j, carry):
        b = lax.rem(gy + j, 16)
        pltpu.make_async_remote_copy(
            src_ref=power.at[pl.ds(pl.multiple_of(b * 16, 16), 16), :],
            dst_ref=landed.at[spot, :],
            send_sem=psend_sem,
            recv_sem=precv_sem,
            device_id=(gx, b),
            device_id_type=MESH,
        ).start()
        return carry

    lax.fori_loop(1, 16, deliver, 0)
    landed[spot, :] = power[spot, :]
    for g in range(GROUPS):
        sent = send.at[pl.ds(0, (Q - 1) * HERE), pl.ds(g * 2 * Q, 2 * Q)]
        pltpu.make_async_copy(sent, sent, send_sem.at[g]).wait()
    pltpu.make_async_copy(power.at[0:240], power.at[0:240], psend_sem).wait()
    pltpu.make_async_copy(landed.at[0:240], landed.at[0:240], precv_sem).wait()
    low = lax.broadcasted_iota(jnp.int32, (16, Q), 1) < K1
    for b in range(0, 16, 2):
        pair = jnp.where(low, landed[b * 16 : b * 16 + 16, :], landed[b * 16 + 16 : b * 16 + 32, :])
        for r in range(NBEAM // 16):
            out[r, :, b * K1 : (b + 2) * K1] = pair[r * TIMES : (r + 1) * TIMES]


def body(voltages, gains, delays, channel_order, beam_table):
    vmem = pl.BlockSpec(memory_space=pltpu.VMEM)
    hbm = pl.BlockSpec(memory_space=pl.ANY)
    return pl.pallas_call(
        kernel,
        out_shape=jax.ShapeDtypeStruct((NBEAM // 16, TIMES, 16 * K1), F32),
        in_specs=[hbm, hbm, vmem, pl.BlockSpec(memory_space=pltpu.SMEM)] + [vmem] * 6,
        out_specs=vmem,
        scratch_shapes=[
            pltpu.VMEM((2, HERE, NCH), F32),
            pltpu.VMEM((Q, Q), jnp.int32),
            pltpu.VMEM((NBEAM, NIN), F32),
            pltpu.VMEM((2 * HERE * KP, Q), F32),
            pltpu.VMEM((HERE * 2 * Q, 2 * Q), BF16),
            pltpu.VMEM((GROUPS, HERE * Q, 2 * Q), BF16),
            pltpu.VMEM((2 * HP * Q, Q), F32),
            pltpu.VMEM((Q * HERE, GROUPS * 2 * Q), BF16),
            pltpu.VMEM((Q * HERE, GROUPS * 2 * Q), BF16),
            pltpu.VMEM((16 * 16, Q), F32),
            pltpu.VMEM((16 * 16, Q), F32),
            pltpu.SMEM((2, Q), jnp.int32),
            pltpu.SemaphoreType.DMA,
            pltpu.SemaphoreType.DMA((GROUPS,)),
            pltpu.SemaphoreType.DMA((GROUPS,)),
            pltpu.SemaphoreType.DMA,
            pltpu.SemaphoreType.DMA,
        ],
        compiler_params=pltpu.CompilerParams(
            collective_id=0, has_side_effects=True, vmem_limit_bytes=60 * 2**20
        ),
    )(voltages, gains, channel_order, beam_table, delays, *tables())


def solution(mesh):
    return jax.shard_map(
        body,
        mesh=mesh,
        in_specs=(P(None, ("gx", "gy"), None), P(None, ("gx", "gy"), None), P(), P(), P()),
        out_specs=P("gy", None, "gx"),
        check_vma=False,
    )
```

time: 110 us -> 78.2 us (0.71)
  Pallas kernels: 102 us -> 76.5 us
  other arithmetic: 3.03 us -> 0 us
  local copies, waits for them, and re-layouts: 4.38 us -> 1.47 us
    pallas_call x1, Pallas kernels: 102 us -> 76.5 us  [body(): pl.pallas_call(kernel, out_shape=jax.ShapeDtypeStruct((NBEAM // 16, TIMES...]
    reshape x2 -> x0, local copies, waits for them, and re-layouts: 2.56 us -> none  [the longest x1 1.34 us: body(): jnp.transpose(landed, (2, 4, 0, 1, 3, 5))]
    select_n x2 -> x0, other arithmetic: 1.55 us -> none  [body(): offsets = jnp.take(delays, beam_table, axis=0)]
    unnamed x2 -> x1, local copies, waits for them, and re-layouts: 0.01 us -> 1.47 us
where the time goes in v2:
time: 78.2 us; the launch traced here: 78 us
  Pallas kernels  76.5 us (98%)
  local copies, waits for them, and re-layouts  1.47 us (2%)
    pallas_call x1, Pallas kernels, body(): pl.pallas_call(kernel, out_shape=jax.ShapeDtypeStruct((NBEAM // 16, TIMES...  76.5 us

profile of v2, /device:TPU:1, one launch (start us, length us, event | category | flops | bytes accessed | tf_op | source)
XLA Modules:
  0.0 78.0 jit_solution(10653896383024763986)
XLA Ops:
  0.0 76.5 %shard_map.100 = f32[4,4,1024]{2,1,0:T(4,128)} custom-call(bf16[2,16,122880]{2,1,0:T(8,128)(2,1)} %volt.1, f32[2,16,8192]{2,1,0:T(8,128)} %gains_hbm.1, s32[8,16]{1,0:T(8,128)} %channel_order.1, s32[64]{0:T(128)} %beam_table.1, f32[64,2048]{1,0:T(8,128)} %delays.1, f32[8,8192]{1,0:T(8,128)} %constant.10.clone.coef, bf16[128,128]{1,0:T(8,128)(2,1)} %constant.11.clone.first, ...), custom_call_target="tpu_custom_call" | custom-call | tf_op jit(solution)/shard_map/pallas_call | solution.py:392
  76.5 1.5 %copy.12 = f32[4,4,1024]{2,1,0:T(4,128)} copy(f32[4,4,1024]{2,1,0:T(4,128)} %shard_map.100) | data formatting | bytes 131072

commit v3 on v2

--- a/solution.py
+++ b/solution.py
@@ -25,7 +25,7 @@
 HERE = 16
 GROUPS = 4
 KK = K1 // GROUPS
-EARLY = 32
+EARLY = 64
 LATE = 2
 PIECES = 4
 PIECE = NCH // PIECES
@@ -43,6 +43,7 @@
     ang = 2 * np.pi / K1 * (k[:, None] * k[None, :] % K1)
     c, s = np.cos(ang), np.sin(ang)
     first = np.block([[c, s], [-s, c]]).astype(np.float32)
+    first = first.reshape(2, GROUPS, KK, 2 * K1).transpose(1, 0, 2, 3).reshape(2 * K1, 2 * K1)
     ang = 2 * np.pi / NCH * (k[:, None] * q[None, :])
     twist = np.stack([np.cos(ang), -np.sin(ang)]).astype(np.float32)
     ang = 2 * np.pi / Q * (q[:, None] * q[None, :] % Q)
@@ -70,6 +71,11 @@
     c = 1 + y * (-1 / 2 + y * (1 / 24 + y * (-1 / 720 + y * (1 / 40320))))
     s = x + x * y * (-1 / 6 + y * (1 / 120 + y * (-1 / 5040 + y * (1 / 362880))))
     return c, s
+
+
+def offsets_in_order():
+    order = [(dx, (b + dx) % 4, (a + b + dx) % 4, core) for a in range(4) for b in range(4) for dx in range(4) for core in range(2)]
+    return order[1:]
 
 
 def kernel(
@@ -90,6 +96,7 @@
     gcol,
     gsel,
     turned,
+    table,
     stage,
     send,
     recv,
@@ -109,121 +116,19 @@
 
     barrier = pltpu.get_barrier_semaphore()
 
-    def greet(a, carry):
-        for b in range(16):
-            pl.semaphore_signal(barrier, inc=1, device_id=(lax.rem(gx + a, 8), b), device_id_type=MESH)
-        return carry
-
-    def plan(m, carry):
-        a, b = lax.div(m, 4), lax.rem(m, 4)
-        for dx in range(4):
-            x = lax.rem(mx + dx, 4)
-            dy = lax.rem(b + dx, 4)
-            y = lax.rem(my + dy, 4)
-            z = lax.rem(mz + a + dy, 4)
-            da = x * 2 + lax.div(y, 2)
-            db = (z * 2 + lax.rem(y, 2)) * 2
-            for core in range(2):
-                target[0, m * 8 + dx * 2 + core] = da
-                target[1, m * 8 + dx * 2 + core] = db + lax.rem(mc + core, 2)
-        return carry
-
-    gains_copy = pltpu.make_async_copy(gains_hbm, gains, gain_sem)
-
-    def filterbank(frames, filt, frame_sem):
-        gains_copy.start()
-        for c in range(PIECES):
-            for f in range(FRAMES):
-                pltpu.make_async_copy(
-                    volt.at[:, :, pl.ds(f * NCH + c * PIECE, PIECE)], frames.at[c, f], frame_sem.at[c]
-                ).start()
-        lax.fori_loop(1, 8, greet, 0)
-        for b in range(1, 16):
-            pl.semaphore_signal(barrier, inc=1, device_id=(gx, lax.rem(gy + b, 16)), device_id_type=MESH)
-        lax.fori_loop(0, 16, plan, 0)
-        owned = [jnp.broadcast_to(channel_order[a : a + 1, :], (16, 16)).astype(F32) + a * 16 for a in range(8)]
-        owned = jnp.concatenate(owned, axis=0)
-        row = lax.broadcasted_iota(jnp.int32, (Q, 16), 0) % 16
-        col = lax.broadcasted_iota(jnp.int32, (Q, 16), 1)
-        owned = jnp.sum(jnp.where(row == col, owned, 0.0), axis=1, keepdims=True)
-        order[...] = jnp.broadcast_to(owned, (Q, Q)).astype(jnp.int32)
-
-        for c in range(PIECES):
-            pltpu.make_async_copy(frames.at[c], frames.at[c], frame_sem.at[c]).wait()
-
-            def fir(a, carry, c=c):
-                here = pl.ds(pl.multiple_of(a * Q, Q), Q)
-                there = pl.ds(pl.multiple_of(c * PIECE + a * Q, Q), Q)
-                taps = [jnp.broadcast_to(coef[pl.ds(t, 1), there], (HERE, Q)) for t in range(TAPS)]
-                for p in range(2):
-                    x = [frames[c, f, p, :, here].astype(F32) for f in range(FRAMES)]
-                    for s in range(NSPEC):
-                        acc = taps[0] * x[s]
-                        for t in range(1, TAPS):
-                            acc = acc + taps[t] * x[s + t]
-                        row = s * HERE * QP + p * K1 + c * (PIECE // Q) + a
-                        filt[pl.ds(row, HERE, stride=QP), :] = acc
-                return carry
-
-            lax.fori_loop(0, PIECE // Q, fir, 0)
-
-        def dft1(n, carry):
-            tc, ts = twist[0], twist[1]
-            for i in (n * 2, n * 2 + 1):
-                for s2 in range(0, NSPEC, 2):
-                    x = [
-                        filt[pl.ds(pl.multiple_of((s * HERE + i) * QP, 8), Q), :].astype(BF16)
-                        for s in (s2, s2 + 1)
-                    ]
-                    inner = jnp.dot(first[...], jnp.concatenate(x, axis=1), preferred_element_type=F32)
-                    for s in range(2):
-                        re = inner[:K1, s * Q : (s + 1) * Q]
-                        im = inner[K1:, s * Q : (s + 1) * Q]
-                        tre = (re * tc - im * ts).astype(BF16)
-                        tim = (re * ts + im * tc).astype(BF16)
-                        for g in range(GROUPS):
-                            rows = pl.ds(pl.multiple_of(i * Q + (s2 + s) * KK, KK), KK)
-                            turned[g, rows, 0:Q] = tre[g * KK : (g + 1) * KK]
-                            turned[g, rows, Q : 2 * Q] = tim[g * KK : (g + 1) * KK]
-            return carry
-
-        lax.fori_loop(0, HERE // 2, dft1, 0)
-
-    pl.run_scoped(
-        filterbank,
-        pltpu.VMEM((PIECES, FRAMES, 2, HERE, PIECE), BF16),
-        pltpu.VMEM((NSPEC * HERE * QP, Q), F32),
-        pltpu.SemaphoreType.DMA((PIECES,)),
-    )
-
-    gains_copy.wait()
-    for j in range(NCH // Q):
-        for p in range(2):
-            gcol[pl.ds(p * HERE * KP + j, HERE, stride=KP), :] = gains[p, :, j * Q : (j + 1) * Q]
-    lane = lax.broadcasted_iota(jnp.int32, (Q, Q), 1)
-    owner = order[...]
-    one_hot = (owner == lane).astype(F32).astype(BF16)
-    half_hot = ((owner // 2) == lane).astype(F32).astype(BF16)[:, :K1]
-    parity = ((owner % 2) == lane // K1).astype(F32)
-    parity = jnp.concatenate([parity, parity], axis=1)
-    table = jnp.dot(one_hot, second[...], preferred_element_type=F32).astype(BF16)
-    table = jnp.concatenate([table[:, : 2 * Q], table[:, 2 * Q :]], axis=0)
-
-    def pick(n, carry):
-        for i in range(4):
-            for p in range(2):
-                at = pl.multiple_of((p * HERE + n * 4 + i) * KP, 8)
-                g = gcol[pl.ds(at, K1), :] * F32(NCH**-0.5)
-                hi = g.astype(BF16)
-                lo = (g - hi.astype(F32)).astype(BF16)
-                both = jnp.dot(half_hot, jnp.concatenate([hi, lo], axis=1), preferred_element_type=F32)
-                at = pl.multiple_of((n * 4 + i) * 2 * Q + p * Q, Q)
-                gsel[pl.ds(at, Q), :] = (both * parity).astype(BF16)
-        return carry
-
-    lax.fori_loop(0, HERE // 4, pick, 0)
-
-    pl.semaphore_wait(barrier, Q - 1)
+    def greet(a, b):
+        pl.semaphore_signal(barrier, inc=1, device_id=(a, b), device_id_type=MESH)
+
+    def plan():
+        xs = [lax.rem(mx + d, 4) * 2 for d in range(4)]
+        ys = [lax.rem(my + d, 4) for d in range(4)]
+        zs = [lax.rem(mz + d, 4) * 4 for d in range(4)]
+        tops = [lax.div(y, 2) for y in ys]
+        lows = [lax.rem(y, 2) * 2 for y in ys]
+        cores = [mc, 1 - mc]
+        for j, (dx, dy, dz, core) in enumerate(offsets_in_order()):
+            target[0, j] = xs[dx] + tops[dy]
+            target[1, j] = zs[dz] + lows[dy] + cores[core]
 
     mine = pl.ds(pl.multiple_of(me * HERE, HERE), HERE)
 
@@ -244,18 +149,18 @@
             hand_out(g, j)
             return carry
 
-        lax.fori_loop(jnp.maximum(start, 1), start + count, one, 0)
-
-    for g in range(GROUPS):
+        lax.fori_loop(start, jnp.minimum(start + count, Q - 1), one, 0)
+
+    def prepare(g):
         cols = slice(g * 2 * Q, (g + 1) * 2 * Q)
 
-        def dft2(ii, carry, g=g):
-            if g:
+        def dft2(ii, carry):
+            if g > 1:
                 hand_out_many(g - 1, ii * EARLY, EARLY)
-            for v in range(2):
-                at = ii * 2 + v
+            for v in range(4):
+                at = ii * 4 + v
                 x = turned[g, pl.ds(pl.multiple_of(at * 2 * Q, 2 * Q), 2 * Q), :]
-                spec = lax.dot_general(table, x, (((1,), (1,)), ((), ())), preferred_element_type=F32)
+                spec = lax.dot_general(table[...], x, (((1,), (1,)), ((), ())), preferred_element_type=F32)
                 gain = jnp.dot(
                     gsel[pl.ds(pl.multiple_of(at * 4 * Q, 4 * Q), 4 * Q), :],
                     spread[:, g * Q : (g + 1) * Q],
@@ -270,9 +175,9 @@
                     stage[pl.ds(Q * HP + at * 2 + u, Q, stride=HP), :] = gr * si + gi * sr
             return carry
 
-        lax.fori_loop(0, HERE // 4, dft2, 0)
-
-        def cast(r, carry, g=g):
+        lax.fori_loop(0, HERE // 8, dft2, 0)
+
+        def cast(r, carry):
             for p in range(2):
                 for w in range(8):
                     rows = pl.ds(pl.multiple_of(r * Q + w * HERE, HERE), HERE)
@@ -282,6 +187,117 @@
 
         lax.fori_loop(0, HERE, cast, 0)
         recv[mine, cols] = send[mine, cols]
+
+    gains_copy = pltpu.make_async_copy(gains_hbm, gains, gain_sem)
+
+    def filterbank(frames, filt, frame_sem):
+        gains_copy.start()
+        for c in range(PIECES):
+            for f in range(FRAMES):
+                pltpu.make_async_copy(
+                    volt.at[:, :, pl.ds(f * NCH + c * PIECE, PIECE)], frames.at[c, f], frame_sem.at[c]
+                ).start()
+        for b in range(1, 16):
+            greet(gx, lax.rem(gy + b, 16))
+
+        def greet_far(far, carry):
+            for b in range(16):
+                greet(lax.rem(gx + far, 8), b)
+            return carry
+
+        lax.fori_loop(1, 8, greet_far, 0)
+        plan()
+        owned = [jnp.broadcast_to(channel_order[a : a + 1, :], (16, 16)).astype(F32) + a * 16 for a in range(8)]
+        owned = jnp.concatenate(owned, axis=0)
+        row = lax.broadcasted_iota(jnp.int32, (Q, 16), 0) % 16
+        col = lax.broadcasted_iota(jnp.int32, (Q, 16), 1)
+        owned = jnp.sum(jnp.where(row == col, owned, 0.0), axis=1, keepdims=True)
+        order[...] = jnp.broadcast_to(owned, (Q, Q)).astype(jnp.int32)
+
+        gains_copy.wait()
+        for j in range(NCH // Q):
+            for p in range(2):
+                gcol[pl.ds(p * HERE * KP + j, HERE, stride=KP), :] = gains[p, :, j * Q : (j + 1) * Q]
+        lane = lax.broadcasted_iota(jnp.int32, (Q, Q), 1)
+        owner = order[...]
+        half_hot = ((owner // 2) == lane).astype(F32).astype(BF16)[:, :K1]
+        parity = ((owner % 2) == lane // K1).astype(F32)
+        parity = jnp.concatenate([parity, parity], axis=1)
+        def pick(n, carry):
+            for i in range(4):
+                for p in range(2):
+                    at = pl.multiple_of((p * HERE + n * 4 + i) * KP, 8)
+                    g = gcol[pl.ds(at, K1), :] * F32(NCH**-0.5)
+                    hi = g.astype(BF16)
+                    lo = (g - hi.astype(F32)).astype(BF16)
+                    both = jnp.dot(half_hot, jnp.concatenate([hi, lo], axis=1), preferred_element_type=F32)
+                    at = pl.multiple_of((n * 4 + i) * 2 * Q + p * Q, Q)
+                    gsel[pl.ds(at, Q), :] = (both * parity).astype(BF16)
+            return carry
+
+        lax.fori_loop(0, HERE // 4, pick, 0)
+
+        for c in range(PIECES):
+            pltpu.make_async_copy(frames.at[c], frames.at[c], frame_sem.at[c]).wait()
+
+            def fir(a, carry, c=c):
+                here = pl.ds(pl.multiple_of(a * Q, Q), Q)
+                there = pl.ds(pl.multiple_of(c * PIECE + a * Q, Q), Q)
+                taps = [jnp.broadcast_to(coef[pl.ds(t, 1), there], (HERE, Q)).astype(BF16) for t in range(TAPS)]
+                for p in range(2):
+                    x = [frames[c, f, p, :, here] for f in range(FRAMES)]
+                    for s in range(NSPEC):
+                        terms = [taps[t] * x[s + t] for t in range(TAPS)]
+                        ends = [terms[t] + terms[TAPS - 1 - t] for t in range(TAPS // 2)]
+                        acc = ends[0] + ends[1] + ends[2] + ends[3]
+                        row = s * HERE * QP + p * K1 + c * (PIECE // Q) + a
+                        filt[pl.ds(row, HERE, stride=QP), :] = acc.astype(F32)
+                return carry
+
+            lax.fori_loop(0, PIECE // Q, fir, 0)
+
+        def dft1(n, carry, low, high):
+            if low:
+                hand_out_many(0, n * (EARLY // 4), EARLY // 4)
+            for i in (n * 2, n * 2 + 1):
+                for s2 in range(0, NSPEC, 2):
+                    x = [
+                        filt[pl.ds(pl.multiple_of((s * HERE + i) * QP, 8), Q), :].astype(BF16)
+                        for s in (s2, s2 + 1)
+                    ]
+                    x = jnp.concatenate(x, axis=1)
+                    inner = jnp.dot(first[low * 2 * KK : high * 2 * KK, :], x, preferred_element_type=F32)
+                    for s in range(2):
+                        for g in range(low, high):
+                            at = (g - low) * 2 * KK
+                            re = inner[at : at + KK, s * Q : (s + 1) * Q]
+                            im = inner[at + KK : at + 2 * KK, s * Q : (s + 1) * Q]
+                            tc = twist[0, g * KK : (g + 1) * KK]
+                            ts = twist[1, g * KK : (g + 1) * KK]
+                            rows = pl.ds(pl.multiple_of(i * Q + (s2 + s) * KK, KK), KK)
+                            turned[g, rows, 0:Q] = (re * tc - im * ts).astype(BF16)
+                            turned[g, rows, Q : 2 * Q] = (re * ts + im * tc).astype(BF16)
+            return carry
+
+        lax.fori_loop(0, HERE // 2, functools.partial(dft1, low=0, high=1), 0)
+        lane = lax.broadcasted_iota(jnp.int32, (Q, Q), 1)
+        one_hot = (order[...] == lane).astype(F32).astype(BF16)
+        rows = jnp.dot(one_hot, second[...], preferred_element_type=F32).astype(BF16)
+        table[0:Q, :] = rows[:, : 2 * Q]
+        table[Q : 2 * Q, :] = rows[:, 2 * Q :]
+        pl.semaphore_wait(barrier, Q - 1)
+        prepare(0)
+        lax.fori_loop(0, HERE // 2, functools.partial(dft1, low=1, high=GROUPS), 0)
+
+    pl.run_scoped(
+        filterbank,
+        pltpu.VMEM((PIECES, FRAMES, 2, HERE, PIECE), BF16),
+        pltpu.VMEM((NSPEC * HERE * QP, Q), F32),
+        pltpu.SemaphoreType.DMA((PIECES,)),
+    )
+
+    for g in range(1, GROUPS):
+        prepare(g)
 
     def beamform(weights):
         centre = order[pl.ds(me, 1), :].astype(F32) * K1 + (K1 - 1) / 2
@@ -401,6 +417,7 @@
             pltpu.VMEM((2 * HERE * KP, Q), F32),
             pltpu.VMEM((HERE * 2 * Q, 2 * Q), BF16),
             pltpu.VMEM((GROUPS, HERE * Q, 2 * Q), BF16),
+            pltpu.VMEM((2 * Q, 2 * Q), BF16),
             pltpu.VMEM((2 * HP * Q, Q), F32),
             pltpu.VMEM((Q * HERE, GROUPS * 2 * Q), BF16),
             pltpu.VMEM((Q * HERE, GROUPS * 2 * Q), BF16),

time: 78.2 us -> 74.3 us (0.950)
  Pallas kernels: 76.5 us -> 72.7 us
    pallas_call x1, Pallas kernels: 76.5 us -> 72.7 us  [body(): pl.pallas_call(kernel, out_shape=jax.ShapeDtypeStruct((NBEAM // 16, TIMES...]
where the time goes in v3:
time: 74.3 us; the launch traced here: 74.2 us
  Pallas kernels  72.7 us (98%)
  local copies, waits for them, and re-layouts  1.47 us (2%)
    pallas_call x1, Pallas kernels, body(): pl.pallas_call(kernel, out_shape=jax.ShapeDtypeStruct((NBEAM // 16, TIMES...  72.7 us

profile of v3, /device:TPU:1, one launch (start us, length us, event | category | flops | bytes accessed | tf_op | source)
XLA Modules:
  0.0 74.2 jit_solution(16085043958387966440)
XLA Ops:
  0.0 72.7 %shard_map.100 = f32[4,4,1024]{2,1,0:T(4,128)} custom-call(bf16[2,16,122880]{2,1,0:T(8,128)(2,1)} %volt.1, f32[2,16,8192]{2,1,0:T(8,128)} %gains_hbm.1, s32[8,16]{1,0:T(8,128)} %channel_order.1, s32[64]{0:T(128)} %beam_table.1, f32[64,2048]{1,0:T(8,128)} %delays.1, f32[8,8192]{1,0:T(8,128)} %constant.10.clone.coef, bf16[128,128]{1,0:T(8,128)(2,1)} %constant.11.clone.first, ...), custom_call_target="tpu_custom_call" | custom-call | tf_op jit(solution)/shard_map/pallas_call | solution.py:408
  72.7 1.5 %copy.12 = f32[4,4,1024]{2,1,0:T(4,128)} copy(f32[4,4,1024]{2,1,0:T(4,128)} %shard_map.100) | data formatting | bytes 131072

commit v4 on v3

--- a/solution.py
+++ b/solution.py
@@ -259,7 +259,8 @@
         def dft1(n, carry, low, high):
             if low:
                 hand_out_many(0, n * (EARLY // 4), EARLY // 4)
-            for i in (n * 2, n * 2 + 1):
+            each = 2 if low else 4
+            for i in [n * each + u for u in range(each)]:
                 for s2 in range(0, NSPEC, 2):
                     x = [
                         filt[pl.ds(pl.multiple_of((s * HERE + i) * QP, 8), Q), :].astype(BF16)
@@ -279,7 +280,7 @@
                             turned[g, rows, Q : 2 * Q] = (re * ts + im * tc).astype(BF16)
             return carry
 
-        lax.fori_loop(0, HERE // 2, functools.partial(dft1, low=0, high=1), 0)
+        lax.fori_loop(0, HERE // 4, functools.partial(dft1, low=0, high=1), 0)
         lane = lax.broadcasted_iota(jnp.int32, (Q, Q), 1)
         one_hot = (order[...] == lane).astype(F32).astype(BF16)
         rows = jnp.dot(one_hot, second[...], preferred_element_type=F32).astype(BF16)

time: 74.3 us -> 73.7 us (level)
  no operation moved by 1% of the time
where the time goes in v4:
time: 73.7 us; the launch traced here: 73.6 us
  Pallas kernels  72.1 us (98%)
  local copies, waits for them, and re-layouts  1.47 us (2%)
    pallas_call x1, Pallas kernels, body(): pl.pallas_call(kernel, out_shape=jax.ShapeDtypeStruct((NBEAM // 16, TIMES...  72.1 us
    unnamed x1, local copies, waits for them, and re-layouts  1.47 us

profile of v4, /device:TPU:1, one launch (start us, length us, event | category | flops | bytes accessed | tf_op | source)
XLA Modules:
  0.0 73.6 jit_solution(15860754907845422998)
XLA Ops:
  0.0 72.1 %shard_map.100 = f32[4,4,1024]{2,1,0:T(4,128)} custom-call(bf16[2,16,122880]{2,1,0:T(8,128)(2,1)} %volt.1, f32[2,16,8192]{2,1,0:T(8,128)} %gains_hbm.1, s32[8,16]{1,0:T(8,128)} %channel_order.1, s32[64]{0:T(128)} %beam_table.1, f32[64,2048]{1,0:T(8,128)} %delays.1, f32[8,8192]{1,0:T(8,128)} %constant.10.clone.coef, bf16[128,128]{1,0:T(8,128)(2,1)} %constant.11.clone.first, ...), custom_call_target="tpu_custom_call" | custom-call | tf_op jit(solution)/shard_map/pallas_call | solution.py:409
  72.1 1.5 %copy.12 = f32[4,4,1024]{2,1,0:T(4,128)} copy(f32[4,4,1024]{2,1,0:T(4,128)} %shard_map.100) | data formatting | bytes 131072
